TPU v7x, 32 devices: a whole 2x2x4 slice. The times are simulated.
32 devices in a mesh: dp: 16 (over z, x, core), tensor: 2 (over y).
Axes of the slice: x: 2, y: 2, z: 4, core: 2. Of those that a mesh axis runs over, the one named last changes fastest.
Arguments:
- master: float32 [2, 16384, 16384], P(None, ('tensor', 'dp')), may hold values from -0.09375 to 0.09375
- tile_order: int32 [2, 64], P('tensor'), may hold values from 0 to 63, each once within a row
- check_weights: int32 [8, 16384], P(None, 'tensor'), may hold values from -7 to 7
Outputs:
- tiled: bfloat16 [2, 16384, 16384], P(None, 'tensor', 'dp')
- checksum: float32 [2, 8, 16384], P(None, None, ('dp', 'tensor'))
Inputs may be any that keep to these rules, and one draw needn't show every extreme that they name: Each row of tile_order lists every number of 0 to 63 once.
All inputs are finite; a program needn't handle non-finite values.
Results may differ from a plain program's by a relative error of at most 0.0029.
Values may be sent and summed in bfloat16 or wider, within the bound.
A program may use at most 192 MiB of HBM per device.

v0:
```python
import jax
import jax.numpy as jnp
from jax import lax
from jax.sharding import PartitionSpec as P

TILE = 128


def on_device(master, tile_order, check_weights):
    tile_rows = TILE
    order = tile_order[0]
    count = order.shape[0]
    low = master.astype(jnp.bfloat16)
    weights = check_weights.astype(jnp.bfloat16)
    received = lax.all_to_all(low, "dp", split_axis=2, concat_axis=1, tiled=True)
    items = received.shape[0]
    columns = received.shape[2]
    blocks = received.reshape(items, count, tile_rows, columns)
    moved = jnp.take(blocks, order, axis=1)
    tiled = moved.reshape(items, count * tile_rows, columns)
    partial_sums = jnp.einsum("cr,lrd->lcd", weights, tiled, preferred_element_type=jnp.float32)
    checksum = lax.psum_scatter(partial_sums, "tensor", scatter_dimension=2, tiled=True)
    return (tiled, checksum)


def solution(mesh):
    in_specs = (P(None, ("tensor", "dp"), None), P("tensor", None), P(None, "tensor"))
    out_specs = (P(None, "tensor", "dp"), P(None, None, ("dp", "tensor")))
    return jax.shard_map(
        on_device, mesh=mesh, in_specs=in_specs, out_specs=out_specs, check_vma=False
    )
```

profile of v0, /device:TPU:0, one launch (start us, length us, event | category | flops | bytes accessed | tf_op | source)
XLA Modules:
  0.0 991.8 jit_solution(9992133989392231566)
XLA Ops:
  7.2 91.2 %copy.8 = bf16[2,512,16384]{1,0,2:T(2,128)(2,1)} copy(f32[2,512,16384]{2,1,0:T(8,128)} %param.3) | data formatting | bytes 100663296 | tf_op args[0]
  98.4 0.0 copy-start.1
  98.4 7.5 all-to-all-start
  105.9 0.0 reduce-scatter.2.cloned.1.call-start
  106.0 0.0 copy-done.1
  106.0 0.1 broadcast_bitcast_fusion
  106.1 588.7 %all-to-all-done = bf16[2,512,16384]{1,0,2:T(2,128)(2,1)} async-done(((bf16[2,512,16384]{1,0,2:T(2,128)(2,1)}), bf16[2,512,16384]{1,0,2:T(2,128)(2,1)}, u32[]{:S(2)}, u32[]{:S(2)}) %all-to-all-start) | async-done | bytes 33554464 | tf_op jit(solution)/shard_map/all_to_all | solution.py:15
  694.8 22.9 %copy.9 = bf16[2,512,16384]{1,2,0:T(8,128)(2,1)} copy(bf16[2,512,16384]{1,0,2:T(2,128)(2,1)} %all-to-all-done) | data formatting | bytes 67108864 | tf_op jit(solution)/shard_map/all_to_all | solution.py:15
  717.8 42.1 %copy.10 = bf16[2,16,512,1024]{3,2,1,0:T(8,128)(2,1)} copy(bf16[2,16,512,1024]{2,3,1,0:T(8,128)(2,1)} %bitcast.23) | data formatting | bytes 67108864 | tf_op jit(solution)/shard_map/all_to_all | solution.py:15
  759.9 23.0 %gather_fusion = bf16[64,2,128,1024]{3,2,1,0:T(8,128)(2,1)} fusion(bf16[2,64,128,1024]{3,2,1,0:T(8,128)(2,1)} %bitcast.21, s32[1024]{0:T(1024)S(1)} %pad_clamp_fusion), kind=kCustom, calls=%fused_computation | custom fusion | bytes 67109120 | tf_op jit(solution)/shard_map/jit(_take)/gather | solution.py:19
  782.9 23.0 %copy.11 = bf16[2,64,128,1024]{3,2,1,0:T(8,128)(2,1)} copy(bf16[2,64,128,1024]{3,2,0,1:T(8,128)(2,1)} %bitcast.22) | data formatting | bytes 67108864 | tf_op jit(solution)/shard_map/jit(_take)/gather | solution.py:19
  805.9 0.0 copy-start
  805.9 22.7 %bitcast_select_fusion = bf16[2,8192,1024]{2,1,0:T(8,128)(2,1)} fusion(bf16[2,64,128,1024]{3,2,1,0:T(8,128)(2,1)} %copy.11, pred[8192]{0:T(1024)(128)(4,1)S(1)} %broadcast_bitcast_fusion), kind=kLoop, calls=%fused_computation.1 | loop fusion | flops 16777216 | bytes 67117056 | tf_op jit(solution)/shard_map/jit(_take)/select_n | solution.py:19
  828.5 0.0 copy-done
  828.5 13.4 %convolution_bitcast_fusion = f32[2,8,1024]{2,1,0:T(8,128)} fusion(bf16[2,8192,1024]{2,1,0:T(8,128)(2,1)} %bitcast_select_fusion, s32[8,8192]{1,0:T(8,128)S(1)} %copy-done), kind=kOutput, calls=%fused_computation.2 | convolution fusion | flops 268500992 | bytes 33882112 | tf_op jit(solution)/shard_map/cr,lrd->lcd/dot_general | solution.py:21
  842.0 0.0 reduce-scatter.2.cloned.1.call-update
  842.0 143.0 %reduce-scatter.2.cloned.1.call-done = f32[2,8,512]{2,1,0:T(8,128)} async-done(((f32[2,8,1024]{2,1,0:T(8,128)}), f32[2,8,512]{2,1,0:T(8,128)}) %reduce-scatter.2.cloned.1.call-update) | async-done | bytes 32784 | tf_op jit(solution)/shard_map/reduce_scatter | solution.py:22
  (3 shorter events, 0.0 us)
Async XLA Ops:
  98.4 7.6 copy-start.1
  98.4 596.4 %all-to-all-start = ((bf16[2,512,16384]{1,0,2:T(2,128)(2,1)}), bf16[2,512,16384]{1,0,2:T(2,128)(2,1)}, u32[]{:S(2)}, u32[]{:S(2)}) async-start(bf16[2,512,16384]{1,0,2:T(2,128)(2,1)} %copy.8), calls=%async_computation | async-start | bytes 67108864 | tf_op jit(solution)/shard_map/all_to_all | solution.py:15
  105.9 879.1 %reduce-scatter.2.cloned.1.call-start = ((), (), s32[]{:S(2)}) async-start(), calls=%async_computation.2 | async-start | bytes 98304 | tf_op jit(solution)/shard_map/reduce_scatter | solution.py:22
  805.9 22.7 %copy-start = (s32[8,8192]{1,0:T(8,128)S(1)}, s32[8,8192]{1,0:T(8,128)}, u32[]{:S(2)}) copy-start(s32[8,8192]{1,0:T(8,128)} %param.5) | copy-start | bytes 786436
Sparse Core Ops, SparseCore 0:
  842.1 142.8 reduce-scatter.1
where the time goes:
time: 995 us; the launch traced here: 992 us
  waiting for transfers between devices  732 us (74%)
  local copies, waits for them, and re-layouts  202 us (20%)
  other arithmetic  22.7 us (2%)
  between operations  14.1 us (1%)
  matrix products  13.4 us (1%)
    all_to_all x1, waiting for transfers between devices, on_device(): lax.all_to_all(low, 'dp', split_axis=2, concat_axis=1, tiled=True)  589 us
    reduce_scatter x1, waiting for transfers between devices, on_device(): lax.psum_scatter(partial_sums, 'tensor', scatter_dimension=2, tiled=True)  143 us
    unnamed x5, local copies, waits for them, and re-layouts  91.2 us
    all_to_all x2, local copies, waits for them, and re-layouts, on_device(): lax.all_to_all(low, 'dp', split_axis=2, concat_axis=1, tiled=True)  65.1 us
    gather x2, local copies, waits for them, and re-layouts, on_device(): moved = jnp.take(blocks, order, axis=1)  46 us
    select_n x2, other arithmetic, on_device(): moved = jnp.take(blocks, order, axis=1)  22.7 us
  transfers between devices with their start and end apart: 2, of which 2 were waited for; matrix products, arithmetic and copies ran while one was open for 0% of the time, Pallas kernels for 0%

commit v1 on v0

v1 whole, which is shorter than its diff:
```python
import functools

import jax
import jax.numpy as jnp
from jax import lax
from jax.experimental import pallas as pl
from jax.experimental.pallas import tpu as pltpu
from jax.sharding import PartitionSpec as P

MESH = pl.DeviceIdType.MESH
TILE = 128
CHUNK = 64
GROUP = 8
VMEM = 58 * 2**20


def exchange_kernel(n, chunk, x, recv, stage, low, in_sem, own_sem, send_sem, recv_sem):
    layers, rows, _ = x.shape
    cols = recv.shape[2]
    per_layer = rows // chunk
    steps = layers * per_layer
    me = lax.axis_index("dp")
    other = lax.axis_index("tensor")

    barrier = pltpu.get_barrier_semaphore()

    def greet(s, carry):
        peer = lax.rem(me + s, n)
        pl.semaphore_signal(barrier, inc=1, device_id=(peer, other), device_id_type=MESH)
        return carry

    lax.fori_loop(1, n, greet, 0)

    def load(c):
        slot = lax.rem(c, 2)
        at = pl.multiple_of(lax.rem(c, per_layer) * chunk, chunk)
        return pltpu.make_async_copy(x.at[c // per_layer, pl.ds(at, chunk)], stage.at[slot], in_sem.at[slot])

    load(0).start()
    pl.semaphore_wait(barrier, n - 1)

    def step(c, carry):
        @pl.when(c + 1 < steps)
        def _():
            load(c + 1).start()

        load(c).wait()
        slot = lax.rem(c, 2)
        layer = c // per_layer
        at = pl.multiple_of(lax.rem(c, per_layer) * chunk, chunk)
        home = pl.multiple_of(me * rows + at, chunk)

        def one(i, carry):
            peer = lax.rem(me + lax.rem(i * 5, n), n)
            src = low.at[peer, layer, pl.ds(at, chunk)]
            src[...] = stage[slot, :, pl.ds(pl.multiple_of(peer * cols, cols), cols)].astype(jnp.bfloat16)

            @pl.when(i < n)
            def _():
                pltpu.make_async_remote_copy(
                    src_ref=src,
                    dst_ref=recv.at[layer, pl.ds(home, chunk)],
                    send_sem=send_sem.at[peer],
                    recv_sem=recv_sem.at[me],
                    device_id=(peer, other),
                    device_id_type=MESH,
                ).start()

            return carry

        lax.fori_loop(1, n + 1, one, 0)
        return carry

    lax.fori_loop(0, steps, step, 0)

    def place(p):
        return recv.at[:, pl.ds(pl.multiple_of(p * rows, rows), rows)]

    own = pltpu.make_async_copy(low.at[me], place(me), own_sem)
    own.start()

    def finish(s, carry):
        peer = lax.rem(me + s, n)
        pltpu.make_async_remote_copy(
            src_ref=low.at[peer],
            dst_ref=place(peer),
            send_sem=send_sem.at[peer],
            recv_sem=recv_sem.at[peer],
            device_id=(peer, other),
            device_id_type=MESH,
        ).wait()
        return carry

    lax.fori_loop(1, n, finish, 0)
    own.wait()


def exchange(n, x):
    layers, rows, width = x.shape
    cols = width // n
    chunk = min(CHUNK, rows)
    return pl.pallas_call(
        functools.partial(exchange_kernel, n, chunk),
        out_shape=jax.ShapeDtypeStruct((layers, n * rows, cols), jnp.bfloat16),
        in_specs=[pl.BlockSpec(memory_space=pl.ANY)],
        out_specs=pl.BlockSpec(memory_space=pl.ANY),
        scratch_shapes=[
            pltpu.VMEM((2, chunk, width), jnp.float32),
            pltpu.VMEM((n, layers, rows, cols), jnp.bfloat16),
            pltpu.SemaphoreType.DMA((2,)),
            pltpu.SemaphoreType.DMA,
            pltpu.SemaphoreType.DMA((n,)),
            pltpu.SemaphoreType.DMA((n,)),
        ],
        compiler_params=pltpu.CompilerParams(collective_id=0, has_side_effects=True, vmem_limit_bytes=VMEM),
        name="exchange",
    )(x)


def place_kernel(order, *refs):
    tiles, (weights, out, sums) = refs[:-3], refs[-3:]
    for i, tile in enumerate(tiles):
        out[0, i * TILE : (i + 1) * TILE, :] = tile[0]
    part = jnp.dot(weights[...], out[0], preferred_element_type=jnp.float32)

    @pl.when(pl.program_id(1) == 0)
    def _():
        sums[0] = part

    @pl.when(pl.program_id(1) > 0)
    def _():
        sums[0] += part


def place_tiles(order, received, weights):
    layers, rows, cols = received.shape
    checks = weights.shape[0]
    count = rows // TILE
    group = min(GROUP, count)

    def tile_at(i):
        return pl.BlockSpec((1, TILE, cols), lambda l, k, order: (l, order[k * group + i], 0))

    return pl.pallas_call(
        place_kernel,
        out_shape=(
            jax.ShapeDtypeStruct((layers, rows, cols), jnp.bfloat16),
            jax.ShapeDtypeStruct((layers, checks, cols), jnp.float32),
        ),
        grid_spec=pltpu.PrefetchScalarGridSpec(
            num_scalar_prefetch=1,
            grid=(layers, count // group),
            in_specs=[tile_at(i) for i in range(group)]
            + [pl.BlockSpec((checks, group * TILE), lambda l, k, order: (0, k))],
            out_specs=(
                pl.BlockSpec((1, group * TILE, cols), lambda l, k, order: (l, k, 0)),
                pl.BlockSpec((1, checks, cols), lambda l, k, order: (l, 0, 0)),
            ),
        ),
        compiler_params=pltpu.CompilerParams(vmem_limit_bytes=VMEM),
        name="place",
    )(order, *([received] * group), weights)


def on_device(n, owners, master, tile_order, check_weights):
    received = exchange(n, master)
    weights = check_weights.astype(jnp.bfloat16)
    tiled, part = place_tiles(tile_order[0], received, weights)
    me = lax.axis_index("tensor")
    width = part.shape[2] // owners

    def share(t):
        return lax.dynamic_slice_in_dim(part, t * width, width, axis=2)

    total = share(me)
    for s in range(1, owners):
        pairs = [(i, (i + s) % owners) for i in range(owners)]
        total += lax.ppermute(share(lax.rem(me + s, owners)), "tensor", pairs)
    return tiled, total


def solution(mesh):
    in_specs = (P(None, ("tensor", "dp"), None), P("tensor", None), P(None, "tensor"))
    out_specs = (P(None, "tensor", "dp"), P(None, None, ("dp", "tensor")))
    return jax.shard_map(
        functools.partial(on_device, mesh.shape["dp"], mesh.shape["tensor"]),
        mesh=mesh,
        in_specs=in_specs,
        out_specs=out_specs,
        check_vma=False,
    )
```

time: 995 us -> 764 us (0.77)
  Pallas kernels: 0 us -> 755 us
  waiting for transfers between devices: 732 us -> 2.39 us
  local copies, waits for them, and re-layouts: 202 us -> 0.77 us
  other arithmetic: 22.7 us -> 2.06 us
  between operations: 14.1 us -> 0.66 us
  matrix products: 13.4 us -> 0 us
    pallas_call x0 -> x2, Pallas kernels: none -> 755 us  [the longest x1 726 us: exchange(): pl.pallas_call(functools.partial(exchange_kernel, n, chunk), out_shape=ja...]
    all_to_all x1 -> x0, waiting for transfers between devices: 589 us -> none  [on_device(): lax.all_to_all(low, 'dp', split_axis=2, concat_axis=1, tiled=True)]
    reduce_scatter x1 -> x0, waiting for transfers between devices: 143 us -> none  [on_device(): lax.psum_scatter(partial_sums, 'tensor', scatter_dimension=2, tiled=True)]
    unnamed x5 -> x2, local copies, waits for them, and re-layouts: 91.2 us -> 0.01 us
    all_to_all x2 -> x0, local copies, waits for them, and re-layouts: 65.1 us -> none  [on_device(): lax.all_to_all(low, 'dp', split_axis=2, concat_axis=1, tiled=True)]
    gather x2 -> x0, local copies, waits for them, and re-layouts: 46 us -> none  [on_device(): moved = jnp.take(blocks, order, axis=1)]
    select_n x2 -> x0, other arithmetic: 22.7 us -> none  [on_device(): moved = jnp.take(blocks, order, axis=1)]
    dot_general x1 -> x0, matrix products: 13.4 us -> none  [on_device(): jnp.einsum('cr,lrd->lcd', weights, tiled, preferred_element_type=jnp.floa...]
  transfers between devices with their start and end apart: 2 -> 1, of which waited for: 2 -> 1; matrix products, arithmetic and copies ran while one was open for 0% -> 0% of each run, Pallas kernels for 0% -> 0%
where the time goes in v1:
time: 764 us; the launch traced here: 763 us
  Pallas kernels  755 us (99%)
    pallas_call x1, Pallas kernels, exchange(): pl.pallas_call(functools.partial(exchange_kernel, n, chunk), out_shape=ja...  726 us
    pallas_call x1, Pallas kernels, place_tiles(): pl.pallas_call(place_kernel, out_shape=(jax.ShapeDtypeStruct((layers, row...  29.4 us
  transfers between devices with their start and end apart: 1, of which 1 were waited for; matrix products, arithmetic and copies ran while one was open for 0% of the time, Pallas kernels for 0%

profile of v1, /device:TPU:0, one launch (start us, length us, event | category | flops | bytes accessed | tf_op | source)
XLA Modules:
  0.0 762.5 jit_solution(16468435169587519132)
XLA Ops:
  0.6 0.0 copy-start
  0.6 725.7 %exchange.1.refs_0_.refs_1_.refs_2_.refs_3_.refs_4_.refs_5_.refs_6_.refs_7_ = bf16[2,8192,1024]{2,1,0:T(8,128)(2,1)} custom-call(f32[2,512,16384]{2,1,0:T(8,128)} %x.1), custom_call_target="tpu_custom_call" | custom-call | tf_op jit(solution)/shard_map/exchange/pallas_call | solution.py:102
  726.3 0.0 copy-done
  726.3 0.7 convert_element_type.3.refs_8_
  727.0 29.4 %place.1 = (bf16[2,8192,1024]{2,1,0:T(8,128)(2,1)}, f32[2,8,1024]{2,1,0:T(8,128)}) custom-call(s32[64]{0:T(128)} %bitcast.1, bf16[2,8192,1024]{2,1,0:T(8,128)(2,1)} %exchange.1.refs_0_.refs_1_.refs_2_.refs_3_.refs_4_.refs_5_.refs_6_.refs_7_, bf16[2,8192,1024]{2,1,0:T(8,128)(2,1)} %exchange.1.refs_0_.refs_1_.refs_2_.refs_3_.refs_4_.refs_5_.refs_6_.refs_7_, ...), custom_call_target="tpu_custom_call" | custom-call | tf_op jit(solution)/shard_map/place/pallas_call | solution.py:144
  756.4 0.8 constant_dynamic-slice_fusion
  757.2 1.5 collective-permute-start
  758.7 2.4 collective-permute-done
  761.1 1.4 dynamic-slice_add_fusion
Async XLA Ops:
  0.6 725.7 %copy-start = (s32[8,8192]{1,0:T(8,128)S(1)}, s32[8,8192]{1,0:T(8,128)}, u32[]{:S(2)}) copy-start(s32[8,8192]{1,0:T(8,128)} %param.5) | copy-start | bytes 786436
  757.2 3.9 collective-permute-start

commit v2 on v1

--- a/solution.py
+++ b/solution.py
@@ -10,7 +10,7 @@
 MESH = pl.DeviceIdType.MESH
 TILE = 128
 CHUNK = 64
-GROUP = 8
+GROUP = 16
 VMEM = 58 * 2**20
 
 

time: 764 us -> 759 us (level)
  no operation moved by 1% of the time
where the time goes in v2:
time: 759 us; the launch traced here: 758 us
  Pallas kernels  750 us (99%)
    pallas_call x1, Pallas kernels, exchange(): pl.pallas_call(functools.partial(exchange_kernel, n, chunk), out_shape=ja...  726 us
    pallas_call x1, Pallas kernels, place_tiles(): pl.pallas_call(place_kernel, out_shape=(jax.ShapeDtypeStruct((layers, row...  24.7 us
  transfers between devices with their start and end apart: 1, of which 1 were waited for; matrix products, arithmetic and copies ran while one was open for 0% of the time, Pallas kernels for 0%

profile of v2, /device:TPU:0, one launch (start us, length us, event | category | flops | bytes accessed | tf_op | source)
XLA Modules:
  0.0 757.8 jit_solution(7975377276993548408)
XLA Ops:
  0.6 0.0 copy-start
  0.6 725.7 %exchange.1.refs_0_.refs_1_.refs_2_.refs_3_.refs_4_.refs_5_.refs_6_.refs_7_.refs_8_.refs_9_.refs_10_.refs_11_.refs_12_.refs_13_.refs_14_.refs_15_ = bf16[2,8192,1024]{2,1,0:T(8,128)(2,1)} custom-call(f32[2,512,16384]{2,1,0:T(8,128)} %x.1), custom_call_target="tpu_custom_call" | custom-call | tf_op jit(solution)/shard_map/exchange/pallas_call | solution.py:102
  726.3 0.0 copy-done
  726.3 0.7 convert_element_type.3.refs_16_
  727.0 24.7 %place.1 = (bf16[2,8192,1024]{2,1,0:T(8,128)(2,1)}, f32[2,8,1024]{2,1,0:T(8,128)}) custom-call(s32[64]{0:T(128)} %bitcast.1, bf16[2,8192,1024]{2,1,0:T(8,128)(2,1)} %exchange.1.refs_0_.refs_1_.refs_2_.refs_3_.refs_4_.refs_5_.refs_6_.refs_7_.refs_8_.refs_9_.refs_10_.refs_11_.refs_12_.refs_13_.refs_14_.refs_15_, ...), custom_call_target="tpu_custom_call" | custom-call | tf_op jit(solution)/shard_map/place/pallas_call | solution.py:144
  751.7 0.8 constant_dynamic-slice_fusion
  752.5 1.5 collective-permute-start
  754.0 2.4 collective-permute-done
  756.4 1.4 dynamic-slice_add_fusion
Async XLA Ops:
  0.6 725.7 %copy-start = (s32[8,8192]{1,0:T(8,128)S(1)}, s32[8,8192]{1,0:T(8,128)}, u32[]{:S(2)}) copy-start(s32[8,8192]{1,0:T(8,128)} %param.5) | copy-start | bytes 786436
  752.5 3.9 collective-permute-start
